TPU v7x, 128 devices: a whole 4x4x4 slice. The times are simulated.
128 devices in a mesh: row: 8 (over z, y_hi), col: 16 (over y_lo, x, core).
Axes of the slice: x: 4, y: 4 (y_hi: 2, y_lo: 2; y = y_hi * 2 + y_lo), z: 4, core: 2. Of those that a mesh axis runs over, the one named last changes fastest.
Arguments:
- traces: bfloat16 [8192, 4, 15000], P('col', None, 'row'), may hold values from -8 to 8
- file_lengths: int32 [16], replicated, may hold values from 1 to 512, 4096 in all
- gap_starts: int32 [16], replicated, may hold values from 0 to 4095
- gap_lengths: int32 [16], replicated, may hold values from 1 to 33
Outputs:
- cross: bfloat16 [32, 2, 4096, 4096], P(None, None, 'row', 'col')
Inputs may be any that keep to these rules, and one draw needn't show every extreme that they name: `file_lengths`: the counts sum to 4096.
All inputs are finite; a program needn't handle non-finite values.
Results may differ from a plain program's by a relative error of at most 0.0071.
Values may be sent and summed in bfloat16 or wider, within the bound.
A program may use at most 128 MiB of HBM per device.

v0:
```python
import math

import jax
import jax.numpy as jnp
from jax import lax
from jax.sharding import PartitionSpec as P

SAMPLES = 15000
BINS = 32


lowest_bin = 60
bin_stride = 15
floor_level = 0.2
half_window = 2


def spread(value, axis, source):
    kept = jnp.where(lax.axis_index(axis) == source, value, 0).astype(value.dtype)
    return lax.psum(kept, axis)


def dft_table(first_sample, sample_count, bin_count, window_length):
    sample = first_sample + lax.iota(jnp.int32, sample_count)
    wave = lowest_bin + bin_stride * lax.iota(jnp.int32, bin_count)
    phase = sample[:, None] * wave[None, :] % window_length
    angle = phase.astype(jnp.float32) * (2.0 * math.pi / window_length)
    taper = 0.5 - 0.5 * jnp.cos(sample.astype(jnp.float32) * (2.0 * math.pi / window_length))
    weight = taper / math.sqrt(window_length)
    table = jnp.concatenate(
        [weight[:, None] * jnp.cos(angle), -weight[:, None] * jnp.sin(angle)], axis=1
    )
    return table.astype(jnp.bfloat16)


def alive(channel, gap_starts, gap_lengths):
    inside = (channel[:, None] >= gap_starts[None, :]) & (
        channel[:, None] < gap_starts[None, :] + gap_lengths[None, :]
    )
    return jnp.where(jnp.any(inside, axis=1), 0.0, 1.0).astype(jnp.float32)


def whiten(spectra, live, bin_count):
    row_count = spectra.shape[0]
    parts = spectra.reshape(row_count, -1, 2, bin_count)
    magnitude = jnp.sqrt(parts[:, :, 0] * parts[:, :, 0] + parts[:, :, 1] * parts[:, :, 1])
    padded = jnp.pad(magnitude, ((0, 0), (0, 0), (half_window, half_window)))
    filled = jnp.pad(jnp.ones((bin_count,), jnp.float32), (half_window, half_window))
    running = padded[:, :, 0:bin_count]
    counted = filled[0:bin_count]
    for offset in range(1, 2 * half_window + 1):
        running = running + padded[:, :, offset : offset + bin_count]
        counted = counted + filled[offset : offset + bin_count]
    level = running / counted
    factor = live[:, None, None] / jnp.maximum(level, floor_level)
    return (parts * factor[:, :, None, :]).reshape(row_count, -1).astype(jnp.bfloat16)


def local(traces, file_lengths, gap_starts, gap_lengths):
    row_total = lax.axis_size("row")
    col_total = lax.axis_size("col")
    row_place = lax.axis_index("row")
    col_place = lax.axis_index("col")
    file_most, window_count, slice_length = traces.shape
    bin_count = BINS
    block_cols = file_most // 2
    channels = block_cols * col_total
    device_count = row_total * col_total
    group_rows = channels // device_count
    table = dft_table(row_place * slice_length, slice_length, bin_count, SAMPLES)
    partial_value = jnp.dot(
        traces.reshape(file_most * window_count, slice_length),
        table,
        preferred_element_type=jnp.float32,
    ).reshape(file_most, window_count * 2 * bin_count)
    features = partial_value.shape[1]
    starts = jnp.cumsum(file_lengths) - file_lengths
    picker = lax.iota(jnp.int32, col_total) == col_place
    my_start = jnp.sum(jnp.where(picker, starts, 0))
    my_length = jnp.sum(jnp.where(picker, file_lengths, 0))
    home_first = (row_place * col_total + col_place) * group_rows
    home_channel = home_first + lax.iota(jnp.int32, group_rows)
    slot_index = lax.iota(jnp.int32, file_most)
    kept = jnp.where((slot_index < my_length)[:, None], partial_value, 0.0)
    canvas = jnp.zeros((channels + file_most, features), jnp.float32)
    canvas = lax.dynamic_update_slice_in_dim(canvas, kept, my_start, 0)[:channels]
    owned = lax.psum_scatter(canvas, ("row", "col"), scatter_dimension=0, tiled=True)
    whitened = whiten(owned, alive(home_channel, gap_starts, gap_lengths), bin_count)
    row_block = lax.all_gather(whitened, "col", axis=0, tiled=True)
    block_rows = row_block.shape[0]
    per_row = col_total // row_total
    halves = row_block.reshape(per_row, block_cols, features)
    offered = lax.dynamic_index_in_dim(halves, col_place % per_row, axis=0, keepdims=False)
    col_block = spread(offered, "row", col_place // per_row)
    left_side = row_block.reshape(block_rows, window_count, 2, bin_count).transpose(3, 0, 1, 2)
    left_side = left_side.reshape(bin_count, block_rows, 2 * window_count)
    right_side = col_block.reshape(block_cols, window_count, 2, bin_count)
    rotated = jnp.stack([-right_side[:, :, 1], right_side[:, :, 0]], axis=2)
    paired = jnp.stack([right_side, rotated], axis=0).transpose(4, 0, 1, 2, 3)
    paired = paired.reshape(bin_count, 2, block_cols, 2 * window_count)
    stacked = jnp.einsum("bik,bqjk->bqij", left_side, paired, preferred_element_type=jnp.float32)
    return (stacked / window_count).astype(jnp.bfloat16)


def solution(mesh):
    in_specs = (P("col", None, "row"), P(), P(), P())
    out_specs = P(None, None, "row", "col")
    return jax.shard_map(local, mesh=mesh, in_specs=in_specs, out_specs=out_specs, check_vma=False)
```

profile of v0, /device:TPU:1, one launch (start us, length us, event | category | flops | bytes accessed | tf_op | source)
XLA Modules:
  0.0 838.3 jit_solution(4916982488993415147)
XLA Ops:
  6.5 0.0 reduce-scatter.2.cloned.1.call-start
  6.5 0.1 subtract_multiply_fusion
  6.6 0.7 copy.34
  7.4 0.1 reduce
  7.5 1.3 fusion.19
  10.1 0.7 iota_compare_fusion
  10.8 16.1 %copy.32 = bf16[512,4,1875]{2,1,0:T(4,128)(2,1)} copy(bf16[512,4,1875]{0,1,2:T(4,128)(2,1)} %param.4) | data formatting | bytes 15360000 | tf_op args[0]
  26.9 13.0 %reshape.96 = bf16[2048,1875]{1,0:T(8,128)(2,1)} reshape(bf16[512,4,1875]{2,1,0:T(4,128)(2,1)} %copy.32) | data formatting | bytes 15360000 | tf_op jit(solution)/shard_map/reshape | solution.py:72
  39.9 1.2 multiply_convert_fusion.2
  41.1 5.7 convolution_bitcast_fusion
  46.8 0.3 copy.33
  47.1 0.3 reshape.97
  48.1 0.1 broadcast_select_fusion
  48.2 2.5 broadcast_in_dim.46
  50.7 0.0 copy-start
  50.7 0.0 copy-start.1
  50.7 3.0 dynamic_update_slice.3
  53.7 4.4 slice.56
  58.0 0.0 reduce-scatter.2.cloned.1.call-update
  58.1 0.0 all-reduce.4.cloned.1.call-start
  58.2 0.0 copy-done
  58.2 0.0 copy-done.1
  58.2 0.1 and_reduce_fusion
  58.3 0.1 fusion.17
  58.4 640.5 %reduce-scatter.2.cloned.1.call-done = f32[32,256]{1,0:T(8,128)} async-done(((f32[4096,256]{1,0:T(8,128)}), f32[32,256]{1,0:T(8,128)}) %reduce-scatter.2.cloned.1.call-update) | async-done | bytes 32784 | tf_op jit(solution)/shard_map/reduce_scatter | solution.py:87
  698.9 0.9 reshape.100
  699.8 0.2 fusion.12
  700.1 0.2 maximum_divide_fusion
  700.3 0.2 mul.116
  700.5 0.8 multiply_convert_fusion.3
  701.3 24.3 %all_gather.3 = bf16[512,256]{1,0:T(8,128)(2,1)S(1)} all-gather(bf16[32,256]{1,0:T(8,128)(2,1)S(1)} %multiply_convert_fusion.3), channel_id=1, replica_groups=mesh['row'=8,'col'=16] {'col'}, dimensions={0}, use_global_device_ids=true | all-gather | bytes 278528 | tf_op jit(solution)/shard_map/all_gather | solution.py:89
  725.5 0.7 select_bitcast_fusion
  726.2 0.0 all-reduce.4.cloned.1.call-update
  726.2 0.1 copy.38
  726.4 73.4 %all-reduce.4.cloned.1.call-done = bf16[256,256]{1,0:T(8,128)(2,1)} async-done(((bf16[256,256]{1,0:T(8,128)(2,1)}), bf16[256,256]{1,0:T(8,128)(2,1)}) %all-reduce.4.cloned.1.call-update) | async-done | bytes 131088 | tf_op jit(solution)/shard_map/psum | solution.py:20
  799.8 1.0 copy.35
  800.9 8.1 fusion
  809.0 22.5 %copy.40 = bf16[32,2,512,256]{3,2,1,0:T(8,128)(2,1)} copy(bf16[32,2,512,256]{2,3,1,0:T(8,128)(2,1)} %fusion) | data formatting | bytes 33554432 | tf_op jit(solution)/shard_map/convert_element_type | solution.py:102
  (10 shorter events, 0.2 us)
Async XLA Ops:
  6.5 692.4 %reduce-scatter.2.cloned.1.call-start = ((), (), s32[]{:S(2)}) async-start(), calls=%async_computation.1 | async-start | bytes 4227072 | tf_op jit(solution)/shard_map/reduce_scatter | solution.py:87
  50.7 7.5 copy-start
  50.7 7.5 copy-start.1
  58.1 741.7 %all-reduce.4.cloned.1.call-start = ((), (), s32[]{:S(2)}) async-start(), calls=%async_computation.2 | async-start | bytes 262144 | tf_op jit(solution)/shard_map/psum | solution.py:20
Sparse Core Ops, SparseCore 0:
  58.2 640.6 reduce-scatter.1
  726.4 73.3 all-reduce.3
where the time goes:
time: 844 us; the launch traced here: 838 us
  waiting for transfers between devices  714 us (85%)
  local copies, waits for them, and re-layouts  65 us (8%)
  blocking collectives  24.3 us (3%)
  between operations  15.5 us (2%)
  matrix products  13.9 us (2%)
    reduce_scatter x1, waiting for transfers between devices, local(): lax.psum_scatter(canvas, ('row', 'col'), scatter_dimension=0, tiled=True)  641 us
    psum x1, waiting for transfers between devices, spread(): return lax.psum(kept, axis)  73.4 us
    all_gather x1, blocking collectives, local(): row_block = lax.all_gather(whitened, 'col', axis=0, tiled=True)  24.3 us
    convert_element_type x1, local copies, waits for them, and re-layouts, local(): return (stacked / window_count).astype(jnp.bfloat16)  22.5 us
  transfers between devices with their start and end apart: 2, of which 2 were waited for; matrix products, arithmetic and copies ran while one was open for 0% of the time, Pallas kernels for 0%

commit v1 on v0

v1 whole, which is shorter than its diff:
```python
import math

import jax
import jax.numpy as jnp
import ml_dtypes
import numpy as np
from jax import lax
from jax.experimental import pallas as pl
from jax.experimental.pallas import tpu as pltpu
from jax.sharding import PartitionSpec as P

SAMPLES = 15000
BINS = 32
WINDOWS = 4
FILE_MOST = 512
N_COL = 16
N_ROW = 8
GAPS = 16
FEATURES = WINDOWS * 2 * BINS
LANES = 128
SLICE = SAMPLES // N_ROW
CHUNKS = 15
CHUNK = SLICE // CHUNKS
AHEAD = 8

lowest_bin = 60
bin_stride = 15
floor_level = 0.2
half_window = 2

VMEM_LIMIT = 60 << 20
MESH = pl.DeviceIdType.MESH


def dft_table():
    sample = np.arange(SAMPLES)
    wave = lowest_bin + bin_stride * np.arange(BINS)
    angle = (sample[:, None] * wave[None, :] % SAMPLES) * (2.0 * math.pi / SAMPLES)
    taper = 0.5 - 0.5 * np.cos(sample * (2.0 * math.pi / SAMPLES))
    weight = taper / math.sqrt(SAMPLES)
    table = np.concatenate([weight[:, None] * np.cos(angle), -weight[:, None] * np.sin(angle)], axis=1)
    table = table.astype(np.float32).astype(ml_dtypes.bfloat16)
    table = table.reshape(N_ROW, CHUNKS, CHUNK, 2 * BINS).transpose(0, 1, 3, 2)
    return np.repeat(table, WINDOWS, axis=3)


def file_bounds(lengths_ref):
    firsts, total = [], 0
    for f in range(N_COL):
        firsts.append(total)
        total = total + lengths_ref[f]
    return firsts + [total]


def dft_kernel(lengths_ref, x_hbm, table_hbm, out_ref, xs, ts, x_sem, t_sem):
    row, col = lax.axis_index("row"), lax.axis_index("col")

    def copies(c):
        return (
            pltpu.make_async_copy(table_hbm.at[row, c], ts.at[c], t_sem.at[c]),
            pltpu.make_async_copy(x_hbm.at[pl.ds(c * CHUNK, CHUNK)], xs.at[c], x_sem.at[c]),
        )

    for c in range(AHEAD):
        for copy in copies(c):
            copy.start()
    first = 0
    for f in range(N_COL):
        first = first + jnp.where(f < col, lengths_ref[f], 0)
    total = None
    for c in range(CHUNKS):
        for copy in copies(c):
            copy.wait()
        if c + AHEAD < CHUNKS:
            for copy in copies(c + AHEAD):
                copy.start()
        table = ts[c]
        window = lax.broadcasted_iota(jnp.int32, table.shape, 1) % WINDOWS
        wide = jnp.concatenate(
            [jnp.where(window == w, table, jnp.zeros_like(table)) for w in range(WINDOWS)], axis=0
        )
        samples = xs[c].reshape(CHUNK * WINDOWS, FILE_MOST)
        part = jnp.dot(wide, samples, preferred_element_type=jnp.float32)
        total = part if total is None else total + part
    turned = pltpu.roll(total, lax.rem(first, FILE_MOST), axis=1)
    for z in range(4):
        for half in range(2):
            out_ref[2 * z + half] = turned[128 * half : 128 * half + 128, LANES * z : LANES * z + LANES]


def whiten(total):
    out = []
    bins = lax.broadcasted_iota(jnp.int32, (BINS, LANES), 0)
    low = jnp.minimum(bins, half_window)
    high = jnp.minimum(BINS - 1 - bins, half_window)
    counted = (low + high + 1).astype(jnp.float32)
    edge = jnp.zeros((8, LANES), jnp.float32)
    for w in range(2):
        re = total[64 * w : 64 * w + BINS]
        im = total[64 * w + BINS : 64 * w + 2 * BINS]
        magnitude = jnp.sqrt(re * re + im * im)
        padded = jnp.concatenate([edge, magnitude, edge], axis=0)
        running = padded[8 - half_window : 8 - half_window + BINS]
        for offset in range(1 - half_window, half_window + 1):
            running = running + padded[8 + offset : 8 + offset + BINS]
        level = running / counted
        factor = 1.0 / jnp.maximum(level, floor_level)
        out.append(jnp.concatenate([re * factor, im * factor], axis=0).astype(jnp.bfloat16))
    return out


def exchange_kernel(
    lengths_ref, gap_starts_ref, gap_lengths_ref, part_ref, left_ref, right_ref,
    sums, white, files, block, rows, cols, send1, recv1, send2, recv2, send3, recv3, send4, recv4, local_sem,
):
    row, col = lax.axis_index("row"), lax.axis_index("col")
    z = row // 2
    half = row % 2
    side = col % 2
    k = col // 2
    barrier = pltpu.get_barrier_semaphore()
    for d in range(1, N_ROW):
        pl.semaphore_signal(barrier, inc=1, device_id=((row + d) % N_ROW, col), device_id_type=MESH)
    for d in range(1, N_COL):
        pl.semaphore_signal(barrier, inc=1, device_id=(row, (col + d) % N_COL), device_id_type=MESH)
    pl.semaphore_wait(barrier, N_ROW + N_COL - 2)

    def copy1(d):
        there = (row + d) % N_ROW
        return pltpu.make_async_remote_copy(
            src_ref=part_ref.at[there], dst_ref=sums.at[d - 1],
            send_sem=send1.at[d - 1], recv_sem=recv1.at[d - 1],
            device_id=(there, col), device_id_type=MESH,
        )

    for d in range(1, N_ROW):
        copy1(d).start()
    channel = FILE_MOST * k + LANES * z + lax.broadcasted_iota(jnp.int32, (1, LANES), 1)
    dead = jnp.zeros((1, LANES), jnp.bool_)
    for g in range(GAPS):
        first = gap_starts_ref[g]
        dead = dead | ((channel >= first) & (channel < first + gap_lengths_ref[g]))
    bounds = file_bounds(lengths_ref)
    total = part_ref[row]
    for d in range(1, N_ROW):
        copy1(d).wait_recv()
        total = total + sums[d - 1]
    pair = whiten(total)
    white[0] = pair[0]
    white[1] = pair[1]

    def copy2(d):
        there = (col + d) % N_COL
        return pltpu.make_async_remote_copy(
            src_ref=white.at[there % 2], dst_ref=files.at[col],
            send_sem=send2.at[d - 1], recv_sem=recv2.at[d - 1],
            device_id=(row, there), device_id_type=MESH,
        )

    for d in range(1, N_COL):
        copy2(d).start()
    files[col] = white[side]
    for d in range(1, N_COL):
        copy2(d).wait_recv()
    chosen = jnp.zeros((64, LANES), jnp.float32)
    for f in range(N_COL):
        mine = (channel >= bounds[f]) & (channel < bounds[f + 1]) & jnp.logical_not(dead)
        chosen = jnp.where(mine, files[f].astype(jnp.float32), chosen)
    block[...] = chosen.astype(jnp.bfloat16)

    at = pl.multiple_of((2 * half + side) * 64, 64)
    lane_block = z % 2
    near = 2 * k + z // 2

    def copy3(d):
        there = (col + d) % N_COL
        return pltpu.make_async_remote_copy(
            src_ref=block, dst_ref=rows.at[z, pl.ds(at, 64)],
            send_sem=send3.at[d], recv_sem=recv3.at[row * 2 + side],
            device_id=(k, there), device_id_type=MESH,
        )

    def copy4(d):
        there = (row + d) % N_ROW
        return pltpu.make_async_remote_copy(
            src_ref=block, dst_ref=cols.at[lane_block, pl.ds(at, 64)],
            send_sem=send4.at[d], recv_sem=recv4.at[lane_block * 4 + half * 2 + side],
            device_id=(there, near), device_id_type=MESH,
        )

    for d in range(1, N_COL):
        copy3(d).start()
    for d in range(1, N_ROW):
        copy4(d).start()

    @pl.when(row != k)
    def _():
        copy3(0).start()

    @pl.when(row == k)
    def _():
        rows[z, pl.ds(at, 64)] = block[...]

    @pl.when(near != col)
    def _():
        copy4(0).start()

    @pl.when(near == col)
    def _():
        cols[lane_block, pl.ds(at, 64)] = block[...]

    for d in range(1, N_ROW):
        copy1(d).wait_send()
    for d in range(1, N_COL):
        copy2(d).wait_send()
        copy3(d).wait_send()
    for d in range(1, N_ROW):
        copy4(d).wait_send()

    @pl.when(row != k)
    def _():
        copy3(0).wait_send()

    @pl.when(near != col)
    def _():
        copy4(0).wait_send()

    for source_row in range(N_ROW):
        for s in range(2):
            @pl.when(jnp.logical_or(row != source_row, col != 2 * row + s))
            def _():
                pltpu.make_async_copy(block, rows.at[0, pl.ds(0, 64)], recv3.at[source_row * 2 + s]).wait()
    for q in range(2):
        for h in range(2):
            for s in range(2):
                @pl.when(jnp.logical_or(row != 2 * (2 * side + q) + h, side != s))
                def _():
                    pltpu.make_async_copy(block, cols.at[0, pl.ds(0, 64)], recv4.at[q * 4 + h * 2 + s]).wait()
    left_ref[...] = rows[...]
    right_ref[...] = cols[...]


def cross_kernel(left_ref, right_ref, out_hbm, left, right, buffer, sem):
    for z in range(4):
        left[LANES * z : LANES * z + LANES, :] = left_ref[z].astype(jnp.float32).T.astype(jnp.bfloat16)
    for q in range(2):
        part = right_ref[q] * jnp.asarray(1.0 / WINDOWS, jnp.bfloat16)
        right[0, :, LANES * q : LANES * q + LANES] = part
        for w in range(WINDOWS):
            re = part[64 * w : 64 * w + BINS]
            im = part[64 * w + BINS : 64 * w + 2 * BINS]
            right[1, 64 * w : 64 * w + BINS, LANES * q : LANES * q + LANES] = -im
            right[1, 64 * w + BINS : 64 * w + 2 * BINS, LANES * q : LANES * q + LANES] = re
    bin_of = lax.broadcasted_iota(jnp.int32, (FEATURES, 2 * LANES), 0) % BINS

    def copy(b):
        return pltpu.make_async_copy(buffer.at[b], out_hbm.at[b], sem.at[b])

    def one_bin(b, carry):
        for q in range(2):
            picked = jnp.where(bin_of == b, right[q], jnp.zeros((), jnp.bfloat16))
            buffer[b, q] = jnp.dot(left[...], picked, preferred_element_type=jnp.float32).astype(jnp.bfloat16)
        copy(b).start()
        return carry

    lax.fori_loop(0, BINS, one_bin, 0, unroll=4)

    def done(b, carry):
        copy(b).wait()
        return carry

    lax.fori_loop(0, BINS, done, 0)


def local(traces, file_lengths, gap_starts, gap_lengths):
    smem = pl.BlockSpec(memory_space=pltpu.SMEM)
    vmem = pl.BlockSpec(memory_space=pltpu.VMEM)
    anywhere = pl.BlockSpec(memory_space=pl.ANY)
    dma = pltpu.SemaphoreType.DMA
    params = dict(vmem_limit_bytes=VMEM_LIMIT)
    table = jnp.asarray(dft_table())
    part = pl.pallas_call(
        dft_kernel,
        out_shape=jax.ShapeDtypeStruct((N_ROW, 128, LANES), jnp.float32),
        in_specs=[smem, anywhere, anywhere],
        out_specs=vmem,
        scratch_shapes=[
            pltpu.VMEM((CHUNKS, CHUNK, WINDOWS, FILE_MOST), jnp.bfloat16),
            pltpu.VMEM((CHUNKS, 2 * BINS, CHUNK * WINDOWS), jnp.bfloat16),
            dma((CHUNKS,)), dma((CHUNKS,)),
        ],
        compiler_params=pltpu.CompilerParams(**params),
        name="table_product",
    )(file_lengths, jnp.transpose(traces, (2, 1, 0)), table)
    left, right = pl.pallas_call(
        exchange_kernel,
        out_shape=(
            jax.ShapeDtypeStruct((4, FEATURES, LANES), jnp.bfloat16),
            jax.ShapeDtypeStruct((2, FEATURES, LANES), jnp.bfloat16),
        ),
        in_specs=[smem, smem, smem, vmem],
        out_specs=(vmem, vmem),
        scratch_shapes=[
            pltpu.VMEM((N_ROW - 1, 128, LANES), jnp.float32),
            pltpu.VMEM((2, 64, LANES), jnp.bfloat16),
            pltpu.VMEM((N_COL, 64, LANES), jnp.bfloat16),
            pltpu.VMEM((64, LANES), jnp.bfloat16),
            pltpu.VMEM((4, FEATURES, LANES), jnp.bfloat16),
            pltpu.VMEM((2, FEATURES, LANES), jnp.bfloat16),
            dma((N_ROW - 1,)), dma((N_ROW - 1,)),
            dma((N_COL - 1,)), dma((N_COL - 1,)),
            dma((N_COL,)), dma((N_COL,)),
            dma((N_ROW,)), dma((N_ROW,)),
            dma,
        ],
        compiler_params=pltpu.CompilerParams(collective_id=0, has_side_effects=True, **params),
        name="exchange",
    )(file_lengths, gap_starts, gap_lengths, part)
    return pl.pallas_call(
        cross_kernel,
        out_shape=jax.ShapeDtypeStruct((BINS, 2, FILE_MOST, 2 * LANES), jnp.bfloat16),
        in_specs=[vmem, vmem],
        out_specs=anywhere,
        scratch_shapes=[
            pltpu.VMEM((FILE_MOST, FEATURES), jnp.bfloat16),
            pltpu.VMEM((2, FEATURES, 2 * LANES), jnp.bfloat16),
            pltpu.VMEM((BINS, 2, FILE_MOST, 2 * LANES), jnp.bfloat16),
            dma((BINS,)),
        ],
        compiler_params=pltpu.CompilerParams(**params),
        name="cross",
    )(left, right)


def solution(mesh):
    in_specs = (P("col", None, "row"), P(), P(), P())
    out_specs = P(None, None, "row", "col")
    return jax.shard_map(local, mesh=mesh, in_specs=in_specs, out_specs=out_specs, check_vma=False)
```

time: 844 us -> 47.4 us (0.06)
  waiting for transfers between devices: 714 us -> 0 us
  local copies, waits for them, and re-layouts: 65 us -> 0 us
  Pallas kernels: 0 us -> 47.2 us
  blocking collectives: 24.3 us -> 0 us
  between operations: 15.5 us -> 0.02 us
  matrix products: 13.9 us -> 0 us
    reduce_scatter x1 -> x0, waiting for transfers between devices: 641 us -> none  [local(): lax.psum_scatter(canvas, ('row', 'col'), scatter_dimension=0, tiled=True)]
    psum x1 -> x0, waiting for transfers between devices: 73.4 us -> none  [spread(): return lax.psum(kept, axis)]
    pallas_call x0 -> x3, Pallas kernels: none -> 47.2 us  [the longest x1 33.1 us: local(): pl.pallas_call(exchange_kernel, out_shape=(jax.ShapeDtypeStruct((4, FEATU...]
    all_gather x1 -> x0, blocking collectives: 24.3 us -> none  [local(): row_block = lax.all_gather(whitened, 'col', axis=0, tiled=True)]
    convert_element_type x1 -> x0, local copies, waits for them, and re-layouts: 22.5 us -> none  [local(): return (stacked / window_count).astype(jnp.bfloat16)]
    unnamed x5 -> x0, local copies, waits for them, and re-layouts: 16.1 us -> none
    reshape x3 -> x0, local copies, waits for them, and re-layouts: 14.2 us -> none  [the longest x1 13 us: local(): traces.reshape(file_most * window_count, slice_length)]
    dot_general x2 -> x0, matrix products: 13.9 us -> none  [the longest x1 8.13 us: local(): jnp.einsum('bik,bqjk->bqij', left_side, paired, preferred_element_type=jn...]
  transfers between devices with their start and end apart: 2 -> 0, of which waited for: 2 -> 0; matrix products, arithmetic and copies ran while one was open for 0% -> 0% of each run, Pallas kernels for 0% -> 0%
where the time goes in v1:
time: 47.4 us; the launch traced here: 47.2 us
  Pallas kernels  47.2 us (100%)
    pallas_call x1, Pallas kernels, local(): pl.pallas_call(exchange_kernel, out_shape=(jax.ShapeDtypeStruct((4, FEATU...  33.1 us
    pallas_call x1, Pallas kernels, local(): pl.pallas_call(cross_kernel, out_shape=jax.ShapeDtypeStruct((BINS, 2, FIL...  8.05 us
    pallas_call x1, Pallas kernels, local(): pl.pallas_call(dft_kernel, out_shape=jax.ShapeDtypeStruct((N_ROW, 128, LA...  6.09 us

profile of v1, /device:TPU:1, one launch (start us, length us, event | category | flops | bytes accessed | tf_op | source)
XLA Modules:
  0.0 47.2 jit_solution(13640192120198853014)
XLA Ops:
  0.0 6.1 %table_product.1.part_ref = f32[8,128,128]{2,1,0:T(8,128)} custom-call(s32[16]{0:T(128)} %lengths_ref.3, bf16[1875,4,512]{2,1,0:T(4,128)(2,1)} %bitcast.1, bf16[8,15,64,500]{3,2,1,0:T(8,128)(2,1)} %constant.2.clone.table_hbm), custom_call_target="tpu_custom_call" | custom-call | tf_op jit(solution)/shard_map/table_product/pallas_call | solution.py:282
  6.1 33.1 %exchange.1 = (bf16[4,256,128]{2,1,0:T(8,128)(2,1)}, bf16[2,256,128]{2,1,0:T(8,128)(2,1)}) custom-call(s32[16]{0:T(128)} %lengths_ref.3, s32[16]{0:T(128)} %gap_starts_ref.1, s32[16]{0:T(128)} %gap_lengths_ref.1, f32[8,128,128]{2,1,0:T(8,128)} %table_product.1.part_ref), custom_call_target="tpu_custom_call" | custom-call | tf_op jit(solution)/shard_map/exchange/pallas_call | solution.py:295
  39.2 8.1 %cross.1 = bf16[32,2,512,256]{3,2,1,0:T(8,128)(2,1)} custom-call(bf16[4,256,128]{2,1,0:T(8,128)(2,1)} %get-tuple-element.7.left_ref, bf16[2,256,128]{2,1,0:T(8,128)(2,1)} %get-tuple-element.8.right_ref), custom_call_target="tpu_custom_call" | custom-call | tf_op jit(solution)/shard_map/cross/pallas_call | solution.py:319

commit v2 on v1

v2 whole, which is shorter than its diff:
```python
import math

import jax
import jax.numpy as jnp
import ml_dtypes
import numpy as np
from jax import lax
from jax.experimental import pallas as pl
from jax.experimental.pallas import tpu as pltpu
from jax.sharding import PartitionSpec as P

SAMPLES = 15000
BINS = 32
WINDOWS = 4
FILE_MOST = 512
N_COL = 16
N_ROW = 8
GAPS = 16
FEATURES = WINDOWS * 2 * BINS
LANES = 128
SLICE = SAMPLES // N_ROW
CHUNKS = 5
CHUNK = SLICE // CHUNKS
AHEAD = 3
TABLE_LANES = -(-CHUNK * WINDOWS // LANES) * LANES

lowest_bin = 60
bin_stride = 15
floor_level = 0.2
half_window = 2

VMEM_LIMIT = 60 << 20
MESH = pl.DeviceIdType.MESH


def dft_table():
    sample = np.arange(SAMPLES)
    wave = lowest_bin + bin_stride * np.arange(BINS)
    angle = (sample[:, None] * wave[None, :] % SAMPLES) * (2.0 * math.pi / SAMPLES)
    taper = 0.5 - 0.5 * np.cos(sample * (2.0 * math.pi / SAMPLES))
    weight = taper / math.sqrt(SAMPLES)
    table = np.concatenate([weight[:, None] * np.cos(angle), -weight[:, None] * np.sin(angle)], axis=1)
    table = table.astype(np.float32).astype(ml_dtypes.bfloat16)
    table = table.reshape(N_ROW, CHUNKS, CHUNK, 2 * BINS).transpose(0, 1, 3, 2)
    table = np.repeat(table, WINDOWS, axis=3)
    return np.pad(table, ((0, 0), (0, 0), (0, 0), (0, TABLE_LANES - CHUNK * WINDOWS)))


def file_bounds(lengths_ref):
    firsts, total = [], 0
    for f in range(N_COL):
        firsts.append(total)
        total = total + lengths_ref[f]
    return firsts + [total]


def whiten(total):
    bins = lax.broadcasted_iota(jnp.int32, (BINS, LANES), 0)
    low = jnp.minimum(bins, half_window)
    high = jnp.minimum(BINS - 1 - bins, half_window)
    counted = (low + high + 1).astype(jnp.float32)
    edge = jnp.zeros((8, LANES), jnp.float32)
    re = total[0:BINS]
    im = total[BINS : 2 * BINS]
    magnitude = jnp.sqrt(re * re + im * im)
    padded = jnp.concatenate([edge, magnitude, edge], axis=0)
    running = padded[8 - half_window : 8 - half_window + BINS]
    for offset in range(1 - half_window, half_window + 1):
        running = running + padded[8 + offset : 8 + offset + BINS]
    level = running / counted
    factor = 1.0 / jnp.maximum(level, floor_level)
    return jnp.concatenate([re * factor, im * factor], axis=0)


def exchange_kernel(
    lengths_ref, gap_starts_ref, gap_lengths_ref, x_hbm, table_hbm, left_ref, right_ref,
    xs, ts, parts, sums, picked, got, block, rows, cols,
    x_sem, t_sem, send1, recv1, send2, recv2, send3, recv3, send4, recv4,
):
    row, col = lax.axis_index("row"), lax.axis_index("col")
    z = row // 2
    half = row % 2
    side = col % 2
    k = col // 2

    def copies(c):
        return (
            pltpu.make_async_copy(table_hbm.at[row, c], ts.at[c], t_sem.at[c]),
            pltpu.make_async_copy(x_hbm.at[pl.ds(c * CHUNK, CHUNK)], xs.at[c], x_sem.at[c]),
        )

    for c in range(AHEAD):
        for copy in copies(c):
            copy.start()

    across = [(d, s) for d in range(N_ROW) for s in range(2) if (d, s) != (0, 0)]

    def row_peer(d, s):
        return (row + d) % N_ROW, 2 * k + (side + s) % 2

    def col_peer(d):
        return row, 2 * ((k + d) % 8) + side

    barrier = pltpu.get_barrier_semaphore()
    for d, s in across:
        pl.semaphore_signal(barrier, inc=1, device_id=row_peer(d, s), device_id_type=MESH)
    for d in range(1, 8):
        pl.semaphore_signal(barrier, inc=1, device_id=col_peer(d), device_id_type=MESH)

    total = None
    for c in range(CHUNKS):
        for copy in copies(c):
            copy.wait()
        if c + AHEAD < CHUNKS:
            for copy in copies(c + AHEAD):
                copy.start()
        table = ts[c, :, 0 : CHUNK * WINDOWS]
        window = lax.broadcasted_iota(jnp.int32, table.shape, 1) % WINDOWS
        wide = jnp.concatenate(
            [jnp.where(window == w, table, jnp.zeros_like(table)) for w in range(WINDOWS)], axis=0
        )
        samples = xs[c].reshape(CHUNK * WINDOWS, FILE_MOST)
        part = jnp.dot(wide, samples, preferred_element_type=jnp.float32)
        total = part if total is None else total + part
    bounds = file_bounds(lengths_ref)
    first = 0
    for f in range(N_COL):
        first = first + jnp.where(f < col, lengths_ref[f], 0)
    turned = pltpu.roll(total, lax.rem(first, FILE_MOST), axis=1)
    for w in range(WINDOWS):
        for q in range(4):
            parts[w, q] = turned[64 * w : 64 * w + 64, LANES * q : LANES * q + LANES]
    pl.semaphore_wait(barrier, len(across) + 7)

    def copy1(i):
        there, lane = row_peer(*across[i])
        window, quarter = 2 * (there % 2) + lane % 2, there // 2
        return pltpu.make_async_remote_copy(
            src_ref=parts.at[window, quarter], dst_ref=sums.at[2 * row + side],
            send_sem=send1.at[i], recv_sem=recv1.at[2 * row + side],
            device_id=(there, lane), device_id_type=MESH,
        )

    for i in range(len(across)):
        copy1(i).start()
    sums[2 * row + side] = parts[2 * half + side, z]
    lane = lax.broadcasted_iota(jnp.int32, (1, LANES), 1)
    low = [0, 0]
    high = [0, 0]
    for f in range(N_COL):
        low[f % 2] = jnp.where(f // 2 == k, bounds[f], low[f % 2])
        high[f % 2] = jnp.where(f // 2 == k, bounds[f + 1], high[f % 2])
    choice = []
    for q in range(8):
        channel = FILE_MOST * q + LANES * z + lane
        dead = jnp.zeros((1, LANES), jnp.bool_)
        for g in range(GAPS):
            gap = gap_starts_ref[g]
            dead = dead | ((channel >= gap) & (channel < gap + gap_lengths_ref[g]))
        live = jnp.where(dead, 0.0, 1.0)
        choice.append([
            jnp.where((channel >= low[s]) & (channel < high[s]), live, 0.0) for s in range(2)
        ])
    for d, s in across:
        there, lane_peer = row_peer(d, s)
        slot = 2 * there + lane_peer % 2
        pltpu.make_async_copy(sums.at[slot], sums.at[slot], recv1.at[slot]).wait()
    white = []
    for s in range(2):
        total = sums[s]
        for r in range(1, N_ROW):
            total = total + sums[2 * r + s]
        white.append(whiten(total))
    for q in range(8):
        merged = jnp.where(choice[q][0] > 0.0, white[0], jnp.where(choice[q][1] > 0.0, white[1], 0.0))
        picked[q] = merged.astype(jnp.bfloat16)

    def copy2(d):
        there = col_peer(d)
        return pltpu.make_async_remote_copy(
            src_ref=picked.at[(k + d) % 8], dst_ref=got.at[k],
            send_sem=send2.at[d - 1], recv_sem=recv2.at[k],
            device_id=there, device_id_type=MESH,
        )

    for d in range(1, 8):
        copy2(d).start()
    got[k] = picked[k]
    for d in range(1, 8):
        slot = (k + d) % 8
        pltpu.make_async_copy(got.at[slot], got.at[slot], recv2.at[slot]).wait()
    whole = got[0].astype(jnp.float32)
    for q in range(1, 8):
        whole = whole + got[q].astype(jnp.float32)
    block[...] = whole.astype(jnp.bfloat16)

    at = pl.multiple_of((2 * half + side) * 64, 64)
    lane_block = z % 2
    near = 2 * k + z // 2

    def copy3(d):
        there = (col + d) % N_COL
        return pltpu.make_async_remote_copy(
            src_ref=block, dst_ref=rows.at[z, pl.ds(at, 64)],
            send_sem=send3.at[d], recv_sem=recv3.at[row * 2 + side],
            device_id=(k, there), device_id_type=MESH,
        )

    def copy4(d):
        there = (row + d) % N_ROW
        return pltpu.make_async_remote_copy(
            src_ref=block, dst_ref=cols.at[lane_block, pl.ds(at, 64)],
            send_sem=send4.at[d], recv_sem=recv4.at[lane_block * 4 + half * 2 + side],
            device_id=(there, near), device_id_type=MESH,
        )

    for d in range(1, N_COL):
        copy3(d).start()
    for d in range(1, N_ROW):
        copy4(d).start()

    @pl.when(row != k)
    def _():
        copy3(0).start()

    @pl.when(row == k)
    def _():
        rows[z, pl.ds(at, 64)] = block[...]

    @pl.when(near != col)
    def _():
        copy4(0).start()

    @pl.when(near == col)
    def _():
        cols[lane_block, pl.ds(at, 64)] = block[...]

    for i in range(len(across)):
        copy1(i).wait_send()
    for d in range(1, 8):
        copy2(d).wait_send()
    for d in range(1, N_COL):
        copy3(d).wait_send()
    for d in range(1, N_ROW):
        copy4(d).wait_send()

    @pl.when(row != k)
    def _():
        copy3(0).wait_send()

    @pl.when(near != col)
    def _():
        copy4(0).wait_send()

    for source_row in range(N_ROW):
        for s in range(2):
            @pl.when(jnp.logical_or(row != source_row, col != 2 * row + s))
            def _():
                pltpu.make_async_copy(block, rows.at[0, pl.ds(0, 64)], recv3.at[source_row * 2 + s]).wait()
    for q in range(2):
        for h in range(2):
            for s in range(2):
                @pl.when(jnp.logical_or(row != 2 * (2 * side + q) + h, side != s))
                def _():
                    pltpu.make_async_copy(block, cols.at[0, pl.ds(0, 64)], recv4.at[q * 4 + h * 2 + s]).wait()
    left_ref[...] = rows[...]
    right_ref[...] = cols[...]


def cross_kernel(left_ref, right_ref, out_hbm, left, right, buffer, sem):
    for z in range(4):
        left[LANES * z : LANES * z + LANES, :] = left_ref[z].astype(jnp.float32).T.astype(jnp.bfloat16)
    for q in range(2):
        part = right_ref[q] * jnp.asarray(1.0 / WINDOWS, jnp.bfloat16)
        right[0, :, LANES * q : LANES * q + LANES] = part
        for w in range(WINDOWS):
            re = part[64 * w : 64 * w + BINS]
            im = part[64 * w + BINS : 64 * w + 2 * BINS]
            right[1, 64 * w : 64 * w + BINS, LANES * q : LANES * q + LANES] = -im
            right[1, 64 * w + BINS : 64 * w + 2 * BINS, LANES * q : LANES * q + LANES] = re
    bin_of = lax.broadcasted_iota(jnp.int32, (FEATURES, 2 * LANES), 0) % BINS

    def copy(b):
        return pltpu.make_async_copy(buffer.at[b], out_hbm.at[b], sem.at[b])

    def one_bin(b, carry):
        for q in range(2):
            picked = jnp.where(bin_of == b, right[q], jnp.zeros((), jnp.bfloat16))
            buffer[b, q] = jnp.dot(left[...], picked, preferred_element_type=jnp.float32).astype(jnp.bfloat16)
        copy(b).start()
        return carry

    lax.fori_loop(0, BINS, one_bin, 0, unroll=4)

    def done(b, carry):
        copy(b).wait()
        return carry

    lax.fori_loop(0, BINS, done, 0)


def local(traces, file_lengths, gap_starts, gap_lengths):
    smem = pl.BlockSpec(memory_space=pltpu.SMEM)
    vmem = pl.BlockSpec(memory_space=pltpu.VMEM)
    anywhere = pl.BlockSpec(memory_space=pl.ANY)
    dma = pltpu.SemaphoreType.DMA
    params = dict(vmem_limit_bytes=VMEM_LIMIT)
    table = jnp.asarray(dft_table())
    left, right = pl.pallas_call(
        exchange_kernel,
        out_shape=(
            jax.ShapeDtypeStruct((4, FEATURES, LANES), jnp.bfloat16),
            jax.ShapeDtypeStruct((2, FEATURES, LANES), jnp.bfloat16),
        ),
        in_specs=[smem, smem, smem, anywhere, anywhere],
        out_specs=(vmem, vmem),
        scratch_shapes=[
            pltpu.VMEM((CHUNKS, CHUNK, WINDOWS, FILE_MOST), jnp.bfloat16),
            pltpu.VMEM((CHUNKS, 2 * BINS, TABLE_LANES), jnp.bfloat16),
            pltpu.VMEM((WINDOWS, 4, 64, LANES), jnp.float32),
            pltpu.VMEM((2 * N_ROW, 64, LANES), jnp.float32),
            pltpu.VMEM((8, 64, LANES), jnp.bfloat16),
            pltpu.VMEM((8, 64, LANES), jnp.bfloat16),
            pltpu.VMEM((64, LANES), jnp.bfloat16),
            pltpu.VMEM((4, FEATURES, LANES), jnp.bfloat16),
            pltpu.VMEM((2, FEATURES, LANES), jnp.bfloat16),
            dma((CHUNKS,)), dma((CHUNKS,)),
            dma((2 * N_ROW - 1,)), dma((2 * N_ROW,)),
            dma((7,)), dma((8,)),
            dma((N_COL,)), dma((N_COL,)),
            dma((N_ROW,)), dma((N_ROW,)),
        ],
        compiler_params=pltpu.CompilerParams(collective_id=0, has_side_effects=True, **params),
        name="exchange",
    )(file_lengths, gap_starts, gap_lengths, jnp.transpose(traces, (2, 1, 0)), table)
    return pl.pallas_call(
        cross_kernel,
        out_shape=jax.ShapeDtypeStruct((BINS, 2, FILE_MOST, 2 * LANES), jnp.bfloat16),
        in_specs=[vmem, vmem],
        out_specs=anywhere,
        scratch_shapes=[
            pltpu.VMEM((FILE_MOST, FEATURES), jnp.bfloat16),
            pltpu.VMEM((2, FEATURES, 2 * LANES), jnp.bfloat16),
            pltpu.VMEM((BINS, 2, FILE_MOST, 2 * LANES), jnp.bfloat16),
            dma((BINS,)),
        ],
        compiler_params=pltpu.CompilerParams(**params),
        name="cross",
    )(left, right)


def solution(mesh):
    in_specs = (P("col", None, "row"), P(), P(), P())
    out_specs = P(None, None, "row", "col")
    return jax.shard_map(local, mesh=mesh, in_specs=in_specs, out_specs=out_specs, check_vma=False)
```

time: 47.4 us -> 40.3 us (0.85)
  Pallas kernels: 47.2 us -> 40.2 us
    pallas_call x1 -> x0, Pallas kernels: 6.09 us -> none  [local(): pl.pallas_call(dft_kernel, out_shape=jax.ShapeDtypeStruct((N_ROW, 128, LA...]
    pallas_call x1, Pallas kernels: 33.1 us -> 32.1 us  [local(): pl.pallas_call(exchange_kernel, out_shape=(jax.ShapeDtypeStruct((4, FEATU...]
where the time goes in v2:
time: 40.3 us; the launch traced here: 40.2 us
  Pallas kernels  40.2 us (100%)
    pallas_call x1, Pallas kernels, local(): pl.pallas_call(exchange_kernel, out_shape=(jax.ShapeDtypeStruct((4, FEATU...  32.1 us
    pallas_call x1, Pallas kernels, local(): pl.pallas_call(cross_kernel, out_shape=jax.ShapeDtypeStruct((BINS, 2, FIL...  8.05 us

profile of v2, /device:TPU:1, one launch (start us, length us, event | category | flops | bytes accessed | tf_op | source)
XLA Modules:
  0.0 40.2 jit_solution(7336022562113798105)
XLA Ops:
  0.0 32.1 %exchange.1 = (bf16[4,256,128]{2,1,0:T(8,128)(2,1)}, bf16[2,256,128]{2,1,0:T(8,128)(2,1)}) custom-call(s32[16]{0:T(128)} %lengths_ref.1, s32[16]{0:T(128)} %gap_starts_ref.1, s32[16]{0:T(128)} %gap_lengths_ref.1, bf16[1875,4,512]{2,1,0:T(4,128)(2,1)} %bitcast.1, bf16[8,5,64,1536]{3,2,1,0:T(8,128)(2,1)} %constant.2.clone.table_hbm), custom_call_target="tpu_custom_call" | custom-call | tf_op jit(solution)/shard_map/exchange/pallas_call | solution.py:309
  32.1 8.1 %cross.1 = bf16[32,2,512,256]{3,2,1,0:T(8,128)(2,1)} custom-call(bf16[4,256,128]{2,1,0:T(8,128)(2,1)} %get-tuple-element.7.left_ref, bf16[2,256,128]{2,1,0:T(8,128)(2,1)} %get-tuple-element.8.right_ref), custom_call_target="tpu_custom_call" | custom-call | tf_op jit(solution)/shard_map/cross/pallas_call | solution.py:336

commit v3 on v2

--- a/solution.py
+++ b/solution.py
@@ -22,6 +22,7 @@
 CHUNKS = 5
 CHUNK = SLICE // CHUNKS
 AHEAD = 3
+HAND_ON = 4
 TABLE_LANES = -(-CHUNK * WINDOWS // LANES) * LANES
 
 lowest_bin = 60
@@ -29,7 +30,8 @@
 floor_level = 0.2
 half_window = 2
 
-VMEM_LIMIT = 60 << 20
+EXCHANGE_VMEM = 48 << 20
+CROSS_VMEM = 24 << 20
 MESH = pl.DeviceIdType.MESH
 
 
@@ -73,9 +75,9 @@
 
 
 def exchange_kernel(
-    lengths_ref, gap_starts_ref, gap_lengths_ref, x_hbm, table_hbm, left_ref, right_ref,
-    xs, ts, parts, sums, picked, got, block, rows, cols,
-    x_sem, t_sem, send1, recv1, send2, recv2, send3, recv3, send4, recv4,
+    lengths_hbm, gap_starts_hbm, gap_lengths_hbm, x_hbm, table_hbm, left_ref, right_ref,
+    lengths_ref, gap_starts_ref, gap_lengths_ref, xs, ts, parts, sums, picked, got, block, rows, cols,
+    small_sem, x_sem, t_sem, send1, recv1, send2, recv2, send3, recv3, send4, recv4, send5, recv5,
 ):
     row, col = lax.axis_index("row"), lax.axis_index("col")
     z = row // 2
@@ -106,6 +108,14 @@
         pl.semaphore_signal(barrier, inc=1, device_id=row_peer(d, s), device_id_type=MESH)
     for d in range(1, 8):
         pl.semaphore_signal(barrier, inc=1, device_id=col_peer(d), device_id_type=MESH)
+
+    small = [
+        pltpu.make_async_copy(lengths_hbm, lengths_ref, small_sem.at[0]),
+        pltpu.make_async_copy(gap_starts_hbm, gap_starts_ref, small_sem.at[1]),
+        pltpu.make_async_copy(gap_lengths_hbm, gap_lengths_ref, small_sem.at[2]),
+    ]
+    for copy in small:
+        copy.start()
 
     total = None
     for c in range(CHUNKS):
@@ -122,6 +132,8 @@
         samples = xs[c].reshape(CHUNK * WINDOWS, FILE_MOST)
         part = jnp.dot(wide, samples, preferred_element_type=jnp.float32)
         total = part if total is None else total + part
+    for copy in small:
+        copy.wait()
     bounds = file_bounds(lengths_ref)
     first = 0
     for f in range(N_COL):
@@ -194,82 +206,91 @@
         whole = whole + got[q].astype(jnp.float32)
     block[...] = whole.astype(jnp.bfloat16)
 
-    at = pl.multiple_of((2 * half + side) * 64, 64)
-    lane_block = z % 2
     near = 2 * k + z // 2
+    at = pl.multiple_of((2 * side + half) * 64, 64)
 
     def copy3(d):
-        there = (col + d) % N_COL
-        return pltpu.make_async_remote_copy(
-            src_ref=block, dst_ref=rows.at[z, pl.ds(at, 64)],
-            send_sem=send3.at[d], recv_sem=recv3.at[row * 2 + side],
-            device_id=(k, there), device_id_type=MESH,
+        return pltpu.make_async_remote_copy(
+            src_ref=block, dst_ref=rows.at[side, z, half],
+            send_sem=send3.at[d], recv_sem=recv3.at[row],
+            device_id=(k, 2 * ((k + d) % 8) + side), device_id_type=MESH,
         )
 
     def copy4(d):
         there = (row + d) % N_ROW
         return pltpu.make_async_remote_copy(
-            src_ref=block, dst_ref=cols.at[lane_block, pl.ds(at, 64)],
-            send_sem=send4.at[d], recv_sem=recv4.at[lane_block * 4 + half * 2 + side],
+            src_ref=block, dst_ref=cols.at[z % 2, pl.ds(at, 64)],
+            send_sem=send4.at[d], recv_sem=recv4.at[(z % 2) * 4 + half * 2 + side],
             device_id=(there, near), device_id_type=MESH,
         )
 
-    for d in range(1, N_COL):
+    def copy5(h):
+        some = rows.at[side, pl.ds(h * HAND_ON, HAND_ON)]
+        return pltpu.make_async_remote_copy(
+            src_ref=some, dst_ref=some, send_sem=send5.at[h], recv_sem=recv5.at[h],
+            device_id=(row, 2 * k + 1 - side), device_id_type=MESH,
+        )
+
+    for d in range(1, 8):
         copy3(d).start()
+
+    @pl.when(row != k)
+    def _():
+        copy3(0).start()
+
+    @pl.when(row == k)
+    def _():
+        rows[side, z, half] = block[...]
+
     for d in range(1, N_ROW):
         copy4(d).start()
 
-    @pl.when(row != k)
-    def _():
-        copy3(0).start()
-
-    @pl.when(row == k)
-    def _():
-        rows[z, pl.ds(at, 64)] = block[...]
-
     @pl.when(near != col)
     def _():
         copy4(0).start()
 
     @pl.when(near == col)
     def _():
-        cols[lane_block, pl.ds(at, 64)] = block[...]
-
-    for i in range(len(across)):
-        copy1(i).wait_send()
-    for d in range(1, 8):
-        copy2(d).wait_send()
-    for d in range(1, N_COL):
-        copy3(d).wait_send()
-    for d in range(1, N_ROW):
-        copy4(d).wait_send()
-
-    @pl.when(row != k)
-    def _():
-        copy3(0).wait_send()
-
-    @pl.when(near != col)
-    def _():
-        copy4(0).wait_send()
-
-    for source_row in range(N_ROW):
-        for s in range(2):
-            @pl.when(jnp.logical_or(row != source_row, col != 2 * row + s))
-            def _():
-                pltpu.make_async_copy(block, rows.at[0, pl.ds(0, 64)], recv3.at[source_row * 2 + s]).wait()
+        cols[z % 2, pl.ds(at, 64)] = block[...]
+
+    for source in range(N_ROW):
+        @pl.when(jnp.logical_or(row != source, k != row))
+        def _():
+            pltpu.make_async_copy(block, rows.at[side, source // 2, source % 2], recv3.at[source]).wait()
+        if source % (2 * HAND_ON) == 2 * HAND_ON - 1:
+            copy5(source // (2 * HAND_ON)).start()
     for q in range(2):
         for h in range(2):
             for s in range(2):
                 @pl.when(jnp.logical_or(row != 2 * (2 * side + q) + h, side != s))
                 def _():
                     pltpu.make_async_copy(block, cols.at[0, pl.ds(0, 64)], recv4.at[q * 4 + h * 2 + s]).wait()
+    right_ref[...] = cols[...]
+    for i in range(len(across)):
+        copy1(i).wait_send()
+    for d in range(1, 8):
+        copy2(d).wait_send()
+        copy3(d).wait_send()
+        copy4(d).wait_send()
+
+    @pl.when(row != k)
+    def _():
+        copy3(0).wait_send()
+
+    @pl.when(near != col)
+    def _():
+        copy4(0).wait_send()
+
+    for h in range(4 // HAND_ON):
+        copy5(h).wait()
     left_ref[...] = rows[...]
-    right_ref[...] = cols[...]
 
 
 def cross_kernel(left_ref, right_ref, out_hbm, left, right, buffer, sem):
     for z in range(4):
-        left[LANES * z : LANES * z + LANES, :] = left_ref[z].astype(jnp.float32).T.astype(jnp.bfloat16)
+        for side in range(2):
+            some = left_ref[side, z].reshape(LANES, LANES).astype(jnp.float32).T.astype(jnp.bfloat16)
+            left[LANES * z : LANES * z + LANES, LANES * side : LANES * side + LANES] = some
     for q in range(2):
         part = right_ref[q] * jnp.asarray(1.0 / WINDOWS, jnp.bfloat16)
         right[0, :, LANES * q : LANES * q + LANES] = part
@@ -290,7 +311,7 @@
         copy(b).start()
         return carry
 
-    lax.fori_loop(0, BINS, one_bin, 0, unroll=4)
+    lax.fori_loop(0, BINS, one_bin, 0, unroll=32)
 
     def done(b, carry):
         copy(b).wait()
@@ -300,21 +321,20 @@
 
 
 def local(traces, file_lengths, gap_starts, gap_lengths):
-    smem = pl.BlockSpec(memory_space=pltpu.SMEM)
     vmem = pl.BlockSpec(memory_space=pltpu.VMEM)
-    anywhere = pl.BlockSpec(memory_space=pl.ANY)
+    anywhere = pl.BlockSpec(memory_space=pltpu.HBM)
     dma = pltpu.SemaphoreType.DMA
-    params = dict(vmem_limit_bytes=VMEM_LIMIT)
     table = jnp.asarray(dft_table())
     left, right = pl.pallas_call(
         exchange_kernel,
         out_shape=(
-            jax.ShapeDtypeStruct((4, FEATURES, LANES), jnp.bfloat16),
+            jax.ShapeDtypeStruct((2, 4, 2, 64, LANES), jnp.bfloat16),
             jax.ShapeDtypeStruct((2, FEATURES, LANES), jnp.bfloat16),
         ),
-        in_specs=[smem, smem, smem, anywhere, anywhere],
+        in_specs=[anywhere] * 5,
         out_specs=(vmem, vmem),
         scratch_shapes=[
+            pltpu.SMEM((N_COL,), jnp.int32), pltpu.SMEM((GAPS,), jnp.int32), pltpu.SMEM((GAPS,), jnp.int32),
             pltpu.VMEM((CHUNKS, CHUNK, WINDOWS, FILE_MOST), jnp.bfloat16),
             pltpu.VMEM((CHUNKS, 2 * BINS, TABLE_LANES), jnp.bfloat16),
             pltpu.VMEM((WINDOWS, 4, 64, LANES), jnp.float32),
@@ -322,17 +342,18 @@
             pltpu.VMEM((8, 64, LANES), jnp.bfloat16),
             pltpu.VMEM((8, 64, LANES), jnp.bfloat16),
             pltpu.VMEM((64, LANES), jnp.bfloat16),
-            pltpu.VMEM((4, FEATURES, LANES), jnp.bfloat16),
+            pltpu.VMEM((2, 4, 2, 64, LANES), jnp.bfloat16),
             pltpu.VMEM((2, FEATURES, LANES), jnp.bfloat16),
-            dma((CHUNKS,)), dma((CHUNKS,)),
+            dma((3,)), dma((CHUNKS,)), dma((CHUNKS,)),
             dma((2 * N_ROW - 1,)), dma((2 * N_ROW,)),
             dma((7,)), dma((8,)),
-            dma((N_COL,)), dma((N_COL,)),
+            dma((8,)), dma((8,)),
             dma((N_ROW,)), dma((N_ROW,)),
+            dma((4 // HAND_ON,)), dma((4 // HAND_ON,)),
         ],
-        compiler_params=pltpu.CompilerParams(collective_id=0, has_side_effects=True, **params),
+        compiler_params=pltpu.CompilerParams(collective_id=0, has_side_effects=True, vmem_limit_bytes=EXCHANGE_VMEM),
         name="exchange",
-    )(file_lengths, gap_starts, gap_lengths, jnp.transpose(traces, (2, 1, 0)), table)
+    )(*[pltpu.with_memory_space_constraint(v, pltpu.HBM) for v in (file_lengths, gap_starts, gap_lengths, jnp.transpose(traces, (2, 1, 0)), table)])
     return pl.pallas_call(
         cross_kernel,
         out_shape=jax.ShapeDtypeStruct((BINS, 2, FILE_MOST, 2 * LANES), jnp.bfloat16),
@@ -344,7 +365,7 @@
             pltpu.VMEM((BINS, 2, FILE_MOST, 2 * LANES), jnp.bfloat16),
             dma((BINS,)),
         ],
-        compiler_params=pltpu.CompilerParams(**params),
+        compiler_params=pltpu.CompilerParams(vmem_limit_bytes=CROSS_VMEM),
         name="cross",
     )(left, right)
 

time: 40.3 us -> 37.2 us (0.923)
  Pallas kernels: 40.2 us -> 37.1 us
    pallas_call x1, Pallas kernels: 8.05 us -> 6.48 us  [local(): pl.pallas_call(cross_kernel, out_shape=jax.ShapeDtypeStruct((BINS, 2, FIL...]
    pallas_call x1, Pallas kernels: 32.1 us -> 30.6 us  [local(): pl.pallas_call(exchange_kernel, out_shape=(jax.ShapeDtypeStruct((2, 4, 2,...]
where the time goes in v3:
time: 37.2 us; the launch traced here: 37.1 us
  Pallas kernels  37.1 us (100%)
    pallas_call x1, Pallas kernels, local(): pl.pallas_call(exchange_kernel, out_shape=(jax.ShapeDtypeStruct((2, 4, 2,...  30.6 us
    pallas_call x1, Pallas kernels, local(): pl.pallas_call(cross_kernel, out_shape=jax.ShapeDtypeStruct((BINS, 2, FIL...  6.48 us

profile of v3, /device:TPU:1, one launch (start us, length us, event | category | flops | bytes accessed | tf_op | source)
XLA Modules:
  0.0 37.1 jit_solution(13955918980576617630)
XLA Ops:
  0.0 30.6 %exchange.1 = (bf16[2,4,2,64,128]{4,3,2,1,0:T(8,128)(2,1)S(1)}, bf16[2,256,128]{2,1,0:T(8,128)(2,1)S(1)}) custom-call(s32[16]{0:T(128)} %lengths_hbm.1, s32[16]{0:T(128)} %gap_starts_hbm.1, s32[16]{0:T(128)} %gap_lengths_hbm.1, bf16[1875,4,512]{2,1,0:T(4,128)(2,1)} %bitcast.1, bf16[8,5,64,1536]{3,2,1,0:T(8,128)(2,1)} %constant.2.clone.table_hbm), custom_call_target="tpu_custom_call" | custom-call | tf_op jit(solution)/shard_map/exchange/pallas_call | solution.py:328
  30.6 6.5 %cross.1 = bf16[32,2,512,256]{3,2,1,0:T(8,128)(2,1)} custom-call(bf16[2,4,2,64,128]{4,3,2,1,0:T(8,128)(2,1)S(1)} %get-tuple-element.7.left_ref, bf16[2,256,128]{2,1,0:T(8,128)(2,1)S(1)} %get-tuple-element.8.right_ref), custom_call_target="tpu_custom_call" | custom-call | tf_op jit(solution)/shard_map/cross/pallas_call | solution.py:357

commit v4 on v3

--- a/solution.py
+++ b/solution.py
@@ -138,24 +138,32 @@
     first = 0
     for f in range(N_COL):
         first = first + jnp.where(f < col, lengths_ref[f], 0)
-    turned = pltpu.roll(total, lax.rem(first, FILE_MOST), axis=1)
+    turn = lax.rem(first, FILE_MOST)
+    pl.semaphore_wait(barrier, len(across) + 7)
+
+    def copy1(w, d):
+        there = 2 * ((z + d) % 4) + w // 2
+        return pltpu.make_async_remote_copy(
+            src_ref=parts.at[w, (z + d) % 4], dst_ref=sums.at[2 * row + side],
+            send_sem=send1.at[4 * w + d], recv_sem=recv1.at[2 * row + side],
+            device_id=(there, 2 * k + w % 2), device_id_type=MESH,
+        )
+
+    own = 2 * half + side
     for w in range(WINDOWS):
+        turned = pltpu.roll(total[64 * w : 64 * w + 64], turn, axis=1)
         for q in range(4):
-            parts[w, q] = turned[64 * w : 64 * w + 64, LANES * q : LANES * q + LANES]
-    pl.semaphore_wait(barrier, len(across) + 7)
-
-    def copy1(i):
-        there, lane = row_peer(*across[i])
-        window, quarter = 2 * (there % 2) + lane % 2, there // 2
-        return pltpu.make_async_remote_copy(
-            src_ref=parts.at[window, quarter], dst_ref=sums.at[2 * row + side],
-            send_sem=send1.at[i], recv_sem=recv1.at[2 * row + side],
-            device_id=(there, lane), device_id_type=MESH,
-        )
-
-    for i in range(len(across)):
-        copy1(i).start()
-    sums[2 * row + side] = parts[2 * half + side, z]
+            parts[w, q] = turned[:, LANES * q : LANES * q + LANES]
+        for d in (1, 3, 2):
+            copy1(w, d).start()
+
+        @pl.when(w != own)
+        def _():
+            copy1(w, 0).start()
+
+        @pl.when(w == own)
+        def _():
+            sums[2 * row + side] = parts[w, z]
     lane = lax.broadcasted_iota(jnp.int32, (1, LANES), 1)
     low = [0, 0]
     high = [0, 0]
@@ -259,15 +267,34 @@
             pltpu.make_async_copy(block, rows.at[side, source // 2, source % 2], recv3.at[source]).wait()
         if source % (2 * HAND_ON) == 2 * HAND_ON - 1:
             copy5(source // (2 * HAND_ON)).start()
+    def turn_block(which):
+        at_lane = pl.ds(pl.multiple_of(LANES * which, LANES), LANES)
+        for q in range(4):
+            some = rows[which, q].reshape(LANES, LANES).astype(jnp.float32)
+            left_ref[LANES * q : LANES * q + LANES, at_lane] = some.T.astype(jnp.bfloat16)
+
+    turn_block(side)
     for q in range(2):
         for h in range(2):
             for s in range(2):
                 @pl.when(jnp.logical_or(row != 2 * (2 * side + q) + h, side != s))
                 def _():
                     pltpu.make_async_copy(block, cols.at[0, pl.ds(0, 64)], recv4.at[q * 4 + h * 2 + s]).wait()
-    right_ref[...] = cols[...]
-    for i in range(len(across)):
-        copy1(i).wait_send()
+    for q in range(2):
+        lanes = pl.ds(LANES * q, LANES)
+        part = cols[q] * jnp.asarray(1.0 / WINDOWS, jnp.bfloat16)
+        right_ref[0, :, lanes] = part
+        for w in range(WINDOWS):
+            right_ref[1, 64 * w : 64 * w + BINS, lanes] = -part[64 * w + BINS : 64 * w + 2 * BINS]
+            right_ref[1, 64 * w + BINS : 64 * w + 2 * BINS, lanes] = part[64 * w : 64 * w + BINS]
+    for w in range(WINDOWS):
+        for d in range(1, 4):
+            copy1(w, d).wait_send()
+
+        @pl.when(w != own)
+        def _():
+            copy1(w, 0).wait_send()
+
     for d in range(1, 8):
         copy2(d).wait_send()
         copy3(d).wait_send()
@@ -283,22 +310,10 @@
 
     for h in range(4 // HAND_ON):
         copy5(h).wait()
-    left_ref[...] = rows[...]
-
-
-def cross_kernel(left_ref, right_ref, out_hbm, left, right, buffer, sem):
-    for z in range(4):
-        for side in range(2):
-            some = left_ref[side, z].reshape(LANES, LANES).astype(jnp.float32).T.astype(jnp.bfloat16)
-            left[LANES * z : LANES * z + LANES, LANES * side : LANES * side + LANES] = some
-    for q in range(2):
-        part = right_ref[q] * jnp.asarray(1.0 / WINDOWS, jnp.bfloat16)
-        right[0, :, LANES * q : LANES * q + LANES] = part
-        for w in range(WINDOWS):
-            re = part[64 * w : 64 * w + BINS]
-            im = part[64 * w + BINS : 64 * w + 2 * BINS]
-            right[1, 64 * w : 64 * w + BINS, LANES * q : LANES * q + LANES] = -im
-            right[1, 64 * w + BINS : 64 * w + 2 * BINS, LANES * q : LANES * q + LANES] = re
+    turn_block(1 - side)
+
+
+def cross_kernel(left_ref, right_ref, out_hbm, buffer, sem):
     bin_of = lax.broadcasted_iota(jnp.int32, (FEATURES, 2 * LANES), 0) % BINS
 
     def copy(b):
@@ -306,8 +321,8 @@
 
     def one_bin(b, carry):
         for q in range(2):
-            picked = jnp.where(bin_of == b, right[q], jnp.zeros((), jnp.bfloat16))
-            buffer[b, q] = jnp.dot(left[...], picked, preferred_element_type=jnp.float32).astype(jnp.bfloat16)
+            picked = jnp.where(bin_of == b, right_ref[q], jnp.zeros((), jnp.bfloat16))
+            buffer[b, q] = jnp.dot(left_ref[...], picked, preferred_element_type=jnp.float32).astype(jnp.bfloat16)
         copy(b).start()
         return carry
 
@@ -328,8 +343,8 @@
     left, right = pl.pallas_call(
         exchange_kernel,
         out_shape=(
-            jax.ShapeDtypeStruct((2, 4, 2, 64, LANES), jnp.bfloat16),
-            jax.ShapeDtypeStruct((2, FEATURES, LANES), jnp.bfloat16),
+            jax.ShapeDtypeStruct((FILE_MOST, FEATURES), jnp.bfloat16),
+            jax.ShapeDtypeStruct((2, FEATURES, 2 * LANES), jnp.bfloat16),
         ),
         in_specs=[anywhere] * 5,
         out_specs=(vmem, vmem),
@@ -345,7 +360,7 @@
             pltpu.VMEM((2, 4, 2, 64, LANES), jnp.bfloat16),
             pltpu.VMEM((2, FEATURES, LANES), jnp.bfloat16),
             dma((3,)), dma((CHUNKS,)), dma((CHUNKS,)),
-            dma((2 * N_ROW - 1,)), dma((2 * N_ROW,)),
+            dma((4 * WINDOWS,)), dma((2 * N_ROW,)),
             dma((7,)), dma((8,)),
             dma((8,)), dma((8,)),
             dma((N_ROW,)), dma((N_ROW,)),
@@ -360,8 +375,6 @@
         in_specs=[vmem, vmem],
         out_specs=anywhere,
         scratch_shapes=[
-            pltpu.VMEM((FILE_MOST, FEATURES), jnp.bfloat16),
-            pltpu.VMEM((2, FEATURES, 2 * LANES), jnp.bfloat16),
             pltpu.VMEM((BINS, 2, FILE_MOST, 2 * LANES), jnp.bfloat16),
             dma((BINS,)),
         ],

time: 37.2 us -> 35 us (0.941)
  Pallas kernels: 37.1 us -> 34.9 us
    pallas_call x1, Pallas kernels: 30.6 us -> 28.5 us  [local(): pl.pallas_call(exchange_kernel, out_shape=(jax.ShapeDtypeStruct((FILE_MOS...]
where the time goes in v4:
time: 35 us; the launch traced here: 34.9 us
  Pallas kernels  34.9 us (100%)
    pallas_call x1, Pallas kernels, local(): pl.pallas_call(exchange_kernel, out_shape=(jax.ShapeDtypeStruct((FILE_MOS...  28.5 us
    pallas_call x1, Pallas kernels, local(): pl.pallas_call(cross_kernel, out_shape=jax.ShapeDtypeStruct((BINS, 2, FIL...  6.38 us

profile of v4, /device:TPU:1, one launch (start us, length us, event | category | flops | bytes accessed | tf_op | source)
XLA Modules:
  0.0 34.9 jit_solution(33979473003760196)
XLA Ops:
  0.0 28.5 %exchange.1 = (bf16[512,256]{1,0:T(8,128)(2,1)S(1)}, bf16[2,256,256]{2,1,0:T(8,128)(2,1)S(1)}) custom-call(s32[16]{0:T(128)} %lengths_hbm.1, s32[16]{0:T(128)} %gap_starts_hbm.1, s32[16]{0:T(128)} %gap_lengths_hbm.1, bf16[1875,4,512]{2,1,0:T(4,128)(2,1)} %bitcast.1, bf16[8,5,64,1536]{3,2,1,0:T(8,128)(2,1)} %constant.2.clone.table_hbm), custom_call_target="tpu_custom_call" | custom-call | tf_op jit(solution)/shard_map/exchange/pallas_call | solution.py:343
  28.5 6.4 %cross.1 = bf16[32,2,512,256]{3,2,1,0:T(8,128)(2,1)} custom-call(bf16[512,256]{1,0:T(8,128)(2,1)S(1)} %get-tuple-element.7.left_ref, bf16[2,256,256]{2,1,0:T(8,128)(2,1)S(1)} %get-tuple-element.8.right_ref), custom_call_target="tpu_custom_call" | custom-call | tf_op jit(solution)/shard_map/cross/pallas_call | solution.py:372

commit v5 on v4

--- a/solution.py
+++ b/solution.py
@@ -150,7 +150,7 @@
         )
 
     own = 2 * half + side
-    for w in range(WINDOWS):
+    for w in (0, 2, 1, 3):
         turned = pltpu.roll(total[64 * w : 64 * w + 64], turn, axis=1)
         for q in range(4):
             parts[w, q] = turned[:, LANES * q : LANES * q + LANES]
@@ -239,8 +239,9 @@
             device_id=(row, 2 * k + 1 - side), device_id_type=MESH,
         )
 
-    for d in range(1, 8):
-        copy3(d).start()
+    for x_step, y_step in ((1, 0), (3, 0), (0, 1), (1, 1), (3, 1), (2, 0), (2, 1)):
+        there = 4 * ((k // 4 + y_step) % 2) + (k % 4 + x_step) % 4
+        copy3(lax.rem(there - k + 8, 8)).start()
 
     @pl.when(row != k)
     def _():

time: 35 us -> 35 us (level)
  no operation moved by 1% of the time
where the time goes in v5:
time: 35 us; the launch traced here: 34.9 us
  Pallas kernels  34.9 us (100%)
    pallas_call x1, Pallas kernels, local(): pl.pallas_call(exchange_kernel, out_shape=(jax.ShapeDtypeStruct((FILE_MOS...  28.5 us
    pallas_call x1, Pallas kernels, local(): pl.pallas_call(cross_kernel, out_shape=jax.ShapeDtypeStruct((BINS, 2, FIL...  6.38 us

profile of v5, /device:TPU:1, one launch (start us, length us, event | category | flops | bytes accessed | tf_op | source)
XLA Modules:
  0.0 34.9 jit_solution(15050255566571772086)
XLA Ops:
  0.0 28.5 %exchange.1 = (bf16[512,256]{1,0:T(8,128)(2,1)S(1)}, bf16[2,256,256]{2,1,0:T(8,128)(2,1)S(1)}) custom-call(s32[16]{0:T(128)} %lengths_hbm.1, s32[16]{0:T(128)} %gap_starts_hbm.1, s32[16]{0:T(128)} %gap_lengths_hbm.1, bf16[1875,4,512]{2,1,0:T(4,128)(2,1)} %bitcast.1, bf16[8,5,64,1536]{3,2,1,0:T(8,128)(2,1)} %constant.2.clone.table_hbm), custom_call_target="tpu_custom_call" | custom-call | tf_op jit(solution)/shard_map/exchange/pallas_call | solution.py:344
  28.5 6.4 %cross.1 = bf16[32,2,512,256]{3,2,1,0:T(8,128)(2,1)} custom-call(bf16[512,256]{1,0:T(8,128)(2,1)S(1)} %get-tuple-element.7.left_ref, bf16[2,256,256]{2,1,0:T(8,128)(2,1)S(1)} %get-tuple-element.8.right_ref), custom_call_target="tpu_custom_call" | custom-call | tf_op jit(solution)/shard_map/cross/pallas_call | solution.py:373

commit v6 on v5

--- a/solution.py
+++ b/solution.py
@@ -317,20 +317,21 @@
 def cross_kernel(left_ref, right_ref, out_hbm, buffer, sem):
     bin_of = lax.broadcasted_iota(jnp.int32, (FEATURES, 2 * LANES), 0) % BINS
 
-    def copy(b):
-        return pltpu.make_async_copy(buffer.at[b], out_hbm.at[b], sem.at[b])
+    def copy(b, q):
+        return pltpu.make_async_copy(buffer.at[b, q], out_hbm.at[b, q], sem.at[b, q])
 
     def one_bin(b, carry):
         for q in range(2):
             picked = jnp.where(bin_of == b, right_ref[q], jnp.zeros((), jnp.bfloat16))
             buffer[b, q] = jnp.dot(left_ref[...], picked, preferred_element_type=jnp.float32).astype(jnp.bfloat16)
-        copy(b).start()
+            copy(b, q).start()
         return carry
 
     lax.fori_loop(0, BINS, one_bin, 0, unroll=32)
 
     def done(b, carry):
-        copy(b).wait()
+        copy(b, 0).wait()
+        copy(b, 1).wait()
         return carry
 
     lax.fori_loop(0, BINS, done, 0)
@@ -377,7 +378,7 @@
         out_specs=anywhere,
         scratch_shapes=[
             pltpu.VMEM((BINS, 2, FILE_MOST, 2 * LANES), jnp.bfloat16),
-            dma((BINS,)),
+            dma((BINS, 2)),
         ],
         compiler_params=pltpu.CompilerParams(vmem_limit_bytes=CROSS_VMEM),
         name="cross",

time: 35 us -> 35.7 us (1.020)
  Pallas kernels: 34.9 us -> 35.6 us
    pallas_call x1, Pallas kernels: 6.38 us -> 7.09 us  [local(): pl.pallas_call(cross_kernel, out_shape=jax.ShapeDtypeStruct((BINS, 2, FIL...]
where the time goes in v6:
time: 35.7 us; the launch traced here: 35.6 us
  Pallas kernels  35.6 us (100%)
    pallas_call x1, Pallas kernels, local(): pl.pallas_call(exchange_kernel, out_shape=(jax.ShapeDtypeStruct((FILE_MOS...  28.5 us
    pallas_call x1, Pallas kernels, local(): pl.pallas_call(cross_kernel, out_shape=jax.ShapeDtypeStruct((BINS, 2, FIL...  7.09 us

profile of v6, /device:TPU:1, one launch (start us, length us, event | category | flops | bytes accessed | tf_op | source)
XLA Modules:
  0.0 35.6 jit_solution(15706670560771688005)
XLA Ops:
  0.0 28.5 %exchange.1 = (bf16[512,256]{1,0:T(8,128)(2,1)S(1)}, bf16[2,256,256]{2,1,0:T(8,128)(2,1)S(1)}) custom-call(s32[16]{0:T(128)} %lengths_hbm.1, s32[16]{0:T(128)} %gap_starts_hbm.1, s32[16]{0:T(128)} %gap_lengths_hbm.1, bf16[1875,4,512]{2,1,0:T(4,128)(2,1)} %bitcast.1, bf16[8,5,64,1536]{3,2,1,0:T(8,128)(2,1)} %constant.2.clone.table_hbm), custom_call_target="tpu_custom_call" | custom-call | tf_op jit(solution)/shard_map/exchange/pallas_call | solution.py:345
  28.5 7.1 %cross.1 = bf16[32,2,512,256]{3,2,1,0:T(8,128)(2,1)} custom-call(bf16[512,256]{1,0:T(8,128)(2,1)S(1)} %get-tuple-element.7.left_ref, bf16[2,256,256]{2,1,0:T(8,128)(2,1)S(1)} %get-tuple-element.8.right_ref), custom_call_target="tpu_custom_call" | custom-call | tf_op jit(solution)/shard_map/cross/pallas_call | solution.py:374
